TPU v7x, 256 devices: a whole 4x4x8 slice. The times are simulated.
256 devices in a mesh: row: 16 (over y, x), col: 16 (over z, core).
Axes of the slice: x: 4, y: 4, z: 8, core: 2. Of those that a mesh axis runs over, the one named last changes fastest.
Arguments:
- slab: float32 [32768, 16384], P('row', 'col'), may hold values from -30 to 30, as said below
- test_matrix: float32 [16384, 128], P('col'), may hold values from -0.046875 to 0.046875
Outputs:
- basis: float32 [32768, 128], P(('row', 'col'))
- r_factor: float32 [128, 128], replicated
Inputs may be any that keep to these rules, and one draw needn't show every extreme that they name: `slab`: the sketch's condition number (largest over smallest singular value) is at most 2000.
All inputs are finite; a program needn't handle non-finite values.
Results may differ from a plain program's by a relative error of at most 0.0003.
Values sent between devices are 32-bit elements; how exact they have to be, the bound alone decides.
No kernel may reach another device: no remote copies, remote signals or barrier semaphores. Data moves between devices by JAX's collectives and lax.ppermute only.
A program may use at most 64 MiB of HBM per device.

v0:
```python
import math
import jax
import jax.numpy as jnp
from jax import lax
from jax.sharding import PartitionSpec as P

HIGHEST = lax.Precision.HIGHEST
CONTRACT = (((0,), (0,)), ((), ()))


def gram_of(matrix):
    return lax.dot_general(
        matrix, matrix, CONTRACT, precision=HIGHEST, preferred_element_type=jnp.float32
    )


def orthonormal(matrix, summed):
    lower_one = jnp.linalg.cholesky(summed(gram_of(matrix)))
    inner = lax.linalg.triangular_solve(
        lower_one, matrix, left_side=False, lower=True, transpose_a=True
    )
    lower_two = jnp.linalg.cholesky(summed(gram_of(inner)))
    result = lax.linalg.triangular_solve(
        lower_two, inner, left_side=False, lower=True, transpose_a=True
    )
    factor = jnp.dot(
        lower_two.T, lower_one.T, precision=HIGHEST, preferred_element_type=jnp.float32
    )
    return (result, factor)


def sum_everywhere(gram):
    return lax.psum(gram, ("row", "col"))


def local(slab, test_matrix):
    row_total = slab.shape[0] * lax.axis_size("row")
    root_rows = math.sqrt(row_total)
    partial_value = jnp.dot(
        slab, test_matrix, precision=HIGHEST, preferred_element_type=jnp.float32
    )
    sketch_one = lax.psum(partial_value, "col")
    pulled_part = lax.dot_general(
        slab, sketch_one, CONTRACT, precision=HIGHEST, preferred_element_type=jnp.float32
    )
    pulled = lax.psum(pulled_part, "row") / row_total
    owned = lax.psum_scatter(
        jnp.dot(slab, pulled, precision=HIGHEST, preferred_element_type=jnp.float32),
        "col",
        scatter_dimension=0,
        tiled=True,
    )
    result, factor = orthonormal(owned, sum_everywhere)
    return (result * root_rows, factor / root_rows)


def solution(mesh):
    in_specs = (P("row", "col"), P("col", None))
    out_specs = (P(("row", "col"), None), P())
    return jax.shard_map(local, mesh=mesh, in_specs=in_specs, out_specs=out_specs, check_vma=False)
```

profile of v0, /device:TPU:1, one launch (start us, length us, event | category | flops | bytes accessed | tf_op | source)
XLA Modules:
  0.0 847.2 jit_solution(4430770114689326085)
XLA Ops:
  7.2 1.0 copy-done
  8.2 9.8 %fusion.22 = f32[2048,128]{1,0:T(8,128)} fusion(f32[2048,1024]{1,0:T(8,128)} %param.5, f32[1024,128]{1,0:T(8,128)S(1)} %copy-done), kind=kOutput, calls=%fused_computation.33 | convolution fusion | flops 3221225472 | bytes 9961472 | tf_op jit(solution)/shard_map/dot_general | solution.py:39
  18.1 115.1 %all-reduce.5.cloned.1.call-done = f32[2048,128]{1,0:T(8,128)} async-done(((f32[2048,128]{1,0:T(8,128)}), f32[2048,128]{1,0:T(8,128)}) %all-reduce.5.cloned.1.call-update) | async-done | bytes 1048592 | tf_op jit(solution)/shard_map/psum | solution.py:42
  133.2 9.2 %convolution_bitcast_fusion.1 = f32[1024,128]{0,1:T(8,128)} fusion(f32[2048,128]{1,0:T(8,128)} %all-reduce.5.cloned.1.call-done, f32[2048,1024]{1,0:T(8,128)} %param.5), kind=kOutput, calls=%fused_computation.1 | convolution fusion | flops 3221225472 | bytes 9961472 | tf_op jit(solution)/shard_map/dot_general | solution.py:43
  142.7 94.3 %all-reduce.7.cloned.1.call-done = f32[1024,128]{0,1:T(8,128)} async-done(((f32[1024,128]{0,1:T(8,128)}), f32[1024,128]{0,1:T(8,128)}) %all-reduce.7.cloned.1.call-update) | async-done | bytes 524304 | tf_op jit(solution)/shard_map/psum | solution.py:46
  236.9 13.0 %convolution_bitcast_fusion = f32[2048,128]{0,1:T(8,128)} fusion(f32[2048,1024]{1,0:T(8,128)} %param.5, f32[1024,128]{0,1:T(8,128)} %all-reduce.7.cloned.1.call-done), kind=kOutput, calls=%fused_computation | convolution fusion | flops 3221356544 | bytes 9961472 | tf_op jit(solution)/shard_map/dot_general | solution.py:48
  250.0 55.4 %reduce-scatter.2.cloned.1.call-done = f32[128,128]{0,1:T(8,128)} async-done(((f32[2048,128]{0,1:T(8,128)}), f32[128,128]{0,1:T(8,128)}) %reduce-scatter.2.cloned.1.call-update) | async-done | bytes 65552 | tf_op jit(solution)/shard_map/reduce_scatter | solution.py:47
  305.3 1.8 fusion.23
  307.4 244.3 %all-reduce.9.cloned.1.call-done = f32[128,128]{0,1:T(8,128)} async-done(((f32[128,128]{0,1:T(8,128)}), f32[128,128]{0,1:T(8,128)}) %all-reduce.9.cloned.1.call-update) | async-done | bytes 65552 | tf_op jit(solution)/shard_map/psum | solution.py:33
  551.7 0.9 copy.5
  552.7 0.9 fusion.6
  553.5 11.7 %cholesky.44 = f32[128,128]{1,0:T(8,128)S(1)} custom-call(f32[128,128]{1,0:T(8,128)S(1)} %fusion.6), custom_call_target="Cholesky" | custom-call | tf_op jit(solution)/shard_map/jit(cholesky)/cholesky | solution.py:18
  566.6 9.8 %custom-call.6 = f32[1,128,128]{1,2,0:T(8,128)S(1)} custom-call(f32[1,128,128]{2,1,0:T(8,128)S(1)} %fusion.10), custom_call_target="InvertDiagBlocksLowerTriangular" | custom-call | tf_op jit(solution)/shard_map/triangular_solve/custom-call.0 | solution.py:19
  576.4 1.1 convolution_bitcast_fusion.3
  577.5 0.9 fusion.24
  578.4 234.2 %all-reduce.11.cloned.1.call-done = f32[128,128]{0,1:T(8,128)} async-done(((f32[128,128]{0,1:T(8,128)}), f32[128,128]{0,1:T(8,128)}) %all-reduce.11.cloned.1.call-update) | async-done | bytes 65552 | tf_op jit(solution)/shard_map/psum | solution.py:33
  812.6 0.9 copy.7
  813.5 0.9 fusion.4
  814.4 11.7 %cholesky.55 = f32[128,128]{1,0:T(8,128)S(1)} custom-call(f32[128,128]{1,0:T(8,128)S(1)} %fusion.4), custom_call_target="Cholesky" | custom-call | tf_op jit(solution)/shard_map/jit(cholesky)/cholesky | solution.py:22
  826.1 0.7 compare_reduce_fusion
  826.9 2.3 convolution_multiply_fusion
  829.1 0.7 select_bitcast_fusion
  829.8 9.8 %custom-call.7 = f32[1,128,128]{1,2,0:T(8,128)S(1)} custom-call(f32[1,128,128]{2,1,0:T(8,128)S(1)} %select_bitcast_fusion), custom_call_target="InvertDiagBlocksLowerTriangular" | custom-call | tf_op jit(solution)/shard_map/triangular_solve/custom-call.0 | solution.py:23
  839.9 0.7 copy.8
  (16 shorter events, 2.4 us)
Async XLA Ops:
  7.2 1.0 copy-start
  7.2 126.1 %all-reduce.5.cloned.1.call-start = ((), (), s32[]{:S(2)}) async-start(), calls=%async_computation.1 | async-start | bytes 2097152 | tf_op jit(solution)/shard_map/psum | solution.py:42
  18.1 218.8 %all-reduce.7.cloned.1.call-start = ((), (), s32[]{:S(2)}) async-start(), calls=%async_computation.2 | async-start | bytes 1048576 | tf_op jit(solution)/shard_map/psum | solution.py:46
  142.4 162.9 %reduce-scatter.2.cloned.1.call-start = ((), (), s32[]{:S(2)}) async-start(), calls=%async_computation.3 | async-start | bytes 1114112 | tf_op jit(solution)/shard_map/reduce_scatter | solution.py:47
  249.9 301.8 %all-reduce.9.cloned.1.call-start = ((), (), s32[]{:S(2)}) async-start(), calls=%async_computation.4 | async-start | bytes 131072 | tf_op jit(solution)/shard_map/psum | solution.py:33
  307.2 505.4 %all-reduce.11.cloned.1.call-start = ((), (), s32[]{:S(2)}) async-start(), calls=%async_computation.5 | async-start | bytes 131072 | tf_op jit(solution)/shard_map/psum | solution.py:33
Sparse Core Ops, SparseCore 0:
  18.2 114.9 all-reduce.4
  142.5 94.3 all-reduce.6
  250.1 55.2 reduce-scatter.1
  312.2 239.4 all-reduce.8
  578.6 234.0 all-reduce.10
where the time goes:
time: 848 us; the launch traced here: 847 us
  waiting for transfers between devices  743 us (88%)
  other arithmetic  47.5 us (6%)
  matrix products  38.4 us (5%)
  between operations  13.9 us (2%)
    psum x2, waiting for transfers between devices, sum_everywhere(): return lax.psum(gram, ('row', 'col'))  478 us
    psum x1, waiting for transfers between devices, local(): sketch_one = lax.psum(partial_value, 'col')  115 us
    psum x1, waiting for transfers between devices, local(): pulled = lax.psum(pulled_part, 'row') / row_total  94.3 us
    reduce_scatter x1, waiting for transfers between devices, local(): lax.psum_scatter(jnp.dot(slab, pulled, precision=HIGHEST, preferred_eleme...  55.4 us
  transfers between devices with their start and end apart: 5, of which 5 were waited for; matrix products, arithmetic and copies ran while one was open for 0% of the time, Pallas kernels for 0%

commit v1 on v0

--- a/solution.py
+++ b/solution.py
@@ -30,7 +30,7 @@
 
 
 def sum_everywhere(gram):
-    return lax.psum(gram, ("row", "col"))
+    return lax.psum(lax.psum(gram, "row"), "col")
 
 
 def local(slab, test_matrix):

time: 848 us -> 755 us (0.89)
  waiting for transfers between devices: 743 us -> 650 us
    psum x2 -> x4, waiting for transfers between devices: 478 us -> 385 us  [sum_everywhere(): return lax.psum(lax.psum(gram, 'row'), 'col')]
  transfers between devices with their start and end apart: 5 -> 7, of which waited for: 5 -> 7; matrix products, arithmetic and copies ran while one was open for 0% -> 0% of each run, Pallas kernels for 0% -> 0%
where the time goes in v1:
time: 755 us
  waiting for transfers between devices  650 us (86%)
  other arithmetic  47.5 us (6%)
  matrix products  38.4 us (5%)
  between operations  14.2 us (2%)
    psum x4, waiting for transfers between devices, sum_everywhere(): return lax.psum(lax.psum(gram, 'row'), 'col')  385 us
    psum x1, waiting for transfers between devices, local(): sketch_one = lax.psum(partial_value, 'col')  115 us
    psum x1, waiting for transfers between devices, local(): pulled = lax.psum(pulled_part, 'row') / row_total  94.3 us
    reduce_scatter x1, waiting for transfers between devices, local(): lax.psum_scatter(jnp.dot(slab, pulled, precision=HIGHEST, preferred_eleme...  55.4 us
  transfers between devices with their start and end apart: 7, of which 7 were waited for; matrix products, arithmetic and copies ran while one was open for 0% of the time, Pallas kernels for 0%

profile of v1, /device:TPU:1, one launch (start us, length us, event | category | flops | bytes accessed | tf_op | source)
XLA Modules:
  0.0 754.8 jit_solution(16160511534034216552)
XLA Ops:
  7.2 1.0 copy-done
  8.2 9.8 %fusion.22 = f32[2048,128]{1,0:T(8,128)} fusion(f32[2048,1024]{1,0:T(8,128)} %param.5, f32[1024,128]{1,0:T(8,128)S(1)} %copy-done), kind=kOutput, calls=%fused_computation.33 | convolution fusion | flops 3221225472 | bytes 9961472 | tf_op jit(solution)/shard_map/dot_general | solution.py:39
  18.1 115.1 %all-reduce.7.cloned.1.call-done = f32[2048,128]{1,0:T(8,128)} async-done(((f32[2048,128]{1,0:T(8,128)}), f32[2048,128]{1,0:T(8,128)}) %all-reduce.7.cloned.1.call-update) | async-done | bytes 1048592 | tf_op jit(solution)/shard_map/psum | solution.py:42
  133.2 9.2 %convolution_bitcast_fusion.1 = f32[1024,128]{0,1:T(8,128)} fusion(f32[2048,128]{1,0:T(8,128)} %all-reduce.7.cloned.1.call-done, f32[2048,1024]{1,0:T(8,128)} %param.5), kind=kOutput, calls=%fused_computation.1 | convolution fusion | flops 3221225472 | bytes 9961472 | tf_op jit(solution)/shard_map/dot_general | solution.py:43
  142.7 94.3 %all-reduce.9.cloned.1.call-done = f32[1024,128]{0,1:T(8,128)} async-done(((f32[1024,128]{0,1:T(8,128)}), f32[1024,128]{0,1:T(8,128)}) %all-reduce.9.cloned.1.call-update) | async-done | bytes 524304 | tf_op jit(solution)/shard_map/psum | solution.py:46
  236.9 13.0 %convolution_bitcast_fusion = f32[2048,128]{0,1:T(8,128)} fusion(f32[2048,1024]{1,0:T(8,128)} %param.5, f32[1024,128]{0,1:T(8,128)} %all-reduce.9.cloned.1.call-done), kind=kOutput, calls=%fused_computation | convolution fusion | flops 3221356544 | bytes 9961472 | tf_op jit(solution)/shard_map/dot_general | solution.py:48
  250.0 55.4 %reduce-scatter.2.cloned.1.call-done = f32[128,128]{0,1:T(8,128)} async-done(((f32[2048,128]{0,1:T(8,128)}), f32[128,128]{0,1:T(8,128)}) %reduce-scatter.2.cloned.1.call-update) | async-done | bytes 65552 | tf_op jit(solution)/shard_map/reduce_scatter | solution.py:47
  305.3 1.8 fusion.23
  307.2 93.0 %all-reduce.11.cloned.1.call-done = f32[128,128]{0,1:T(8,128)} async-done(((f32[128,128]{0,1:T(8,128)}), f32[128,128]{0,1:T(8,128)}) %all-reduce.11.cloned.1.call-update) | async-done | bytes 65552 | tf_op jit(solution)/shard_map/psum | solution.py:33
  400.5 102.2 %all-reduce.13.cloned.1.call-done = f32[128,128]{0,1:T(8,128)} async-done(((f32[128,128]{0,1:T(8,128)}), f32[128,128]{0,1:T(8,128)}) %all-reduce.13.cloned.1.call-update) | async-done | bytes 65552 | tf_op jit(solution)/shard_map/psum | solution.py:33
  502.7 0.9 copy.5
  503.6 0.9 fusion.6
  504.5 11.7 %cholesky.44 = f32[128,128]{1,0:T(8,128)S(1)} custom-call(f32[128,128]{1,0:T(8,128)S(1)} %fusion.6), custom_call_target="Cholesky" | custom-call | tf_op jit(solution)/shard_map/jit(cholesky)/cholesky | solution.py:18
  517.6 9.8 %custom-call.6 = f32[1,128,128]{1,2,0:T(8,128)S(1)} custom-call(f32[1,128,128]{2,1,0:T(8,128)S(1)} %fusion.10), custom_call_target="InvertDiagBlocksLowerTriangular" | custom-call | tf_op jit(solution)/shard_map/triangular_solve/custom-call.0 | solution.py:19
  527.4 1.1 convolution_bitcast_fusion.3
  528.5 0.9 fusion.24
  529.7 87.5 %all-reduce.15.cloned.1.call-done = f32[128,128]{0,1:T(8,128)} async-done(((f32[128,128]{0,1:T(8,128)}), f32[128,128]{0,1:T(8,128)}) %all-reduce.15.cloned.1.call-update) | async-done | bytes 65552 | tf_op jit(solution)/shard_map/psum | solution.py:33
  617.2 102.6 %all-reduce.17.cloned.1.call-done = f32[128,128]{0,1:T(8,128)} async-done(((f32[128,128]{0,1:T(8,128)}), f32[128,128]{0,1:T(8,128)}) %all-reduce.17.cloned.1.call-update) | async-done | bytes 65552 | tf_op jit(solution)/shard_map/psum | solution.py:33
  719.8 0.9 copy.7
  720.8 0.9 fusion.4
  721.6 11.7 %cholesky.55 = f32[128,128]{1,0:T(8,128)S(1)} custom-call(f32[128,128]{1,0:T(8,128)S(1)} %fusion.4), custom_call_target="Cholesky" | custom-call | tf_op jit(solution)/shard_map/jit(cholesky)/cholesky | solution.py:22
  734.1 2.3 convolution_multiply_fusion
  737.1 9.8 %custom-call.7 = f32[1,128,128]{1,2,0:T(8,128)S(1)} custom-call(f32[1,128,128]{2,1,0:T(8,128)S(1)} %select_bitcast_fusion), custom_call_target="InvertDiagBlocksLowerTriangular" | custom-call | tf_op jit(solution)/shard_map/triangular_solve/custom-call.0 | solution.py:23
  747.2 0.7 copy.8
  (22 shorter events, 4.2 us)
Async XLA Ops:
  7.2 1.0 copy-start
  7.2 126.1 %all-reduce.7.cloned.1.call-start = ((), (), s32[]{:S(2)}) async-start(), calls=%async_computation.1 | async-start | bytes 2097152 | tf_op jit(solution)/shard_map/psum | solution.py:42
  18.1 218.8 %all-reduce.9.cloned.1.call-start = ((), (), s32[]{:S(2)}) async-start(), calls=%async_computation.2 | async-start | bytes 1048576 | tf_op jit(solution)/shard_map/psum | solution.py:46
  142.4 162.9 %reduce-scatter.2.cloned.1.call-start = ((), (), s32[]{:S(2)}) async-start(), calls=%async_computation.3 | async-start | bytes 1114112 | tf_op jit(solution)/shard_map/reduce_scatter | solution.py:47
  249.9 150.3 %all-reduce.11.cloned.1.call-start = ((), (), s32[]{:S(2)}) async-start(), calls=%async_computation.4 | async-start | bytes 131072 | tf_op jit(solution)/shard_map/psum | solution.py:33
  307.2 195.5 %all-reduce.13.cloned.1.call-start = ((), (), s32[]{:S(2)}) async-start(), calls=%async_computation.5 | async-start | bytes 131072 | tf_op jit(solution)/shard_map/psum | solution.py:33
  400.2 217.0 %all-reduce.15.cloned.1.call-start = ((), (), s32[]{:S(2)}) async-start(), calls=%async_computation.6 | async-start | bytes 131072 | tf_op jit(solution)/shard_map/psum | solution.py:33
  529.4 190.4 %all-reduce.17.cloned.1.call-start = ((), (), s32[]{:S(2)}) async-start(), calls=%async_computation.7 | async-start | bytes 131072 | tf_op jit(solution)/shard_map/psum | solution.py:33
Sparse Core Ops, SparseCore 0:
  18.2 114.9 all-reduce.6
  142.5 94.3 all-reduce.8
  250.1 55.2 reduce-scatter.1
  309.3 90.8 all-reduce.10
  402.4 100.2 all-reduce.12
  529.5 87.6 all-reduce.14
  619.5 100.2 all-reduce.16

commit v2 on v0

--- a/solution.py
+++ b/solution.py
@@ -39,7 +39,11 @@
     partial_value = jnp.dot(
         slab, test_matrix, precision=HIGHEST, preferred_element_type=jnp.float32
     )
-    sketch_one = lax.psum(partial_value, "col")
+    sketch_one = partial_value
+    for hop in (1, 2, 4, 8):
+        sketch_one = sketch_one + lax.ppermute(
+            sketch_one, "col", [(dev, dev ^ hop) for dev in range(16)]
+        )
     pulled_part = lax.dot_general(
         slab, sketch_one, CONTRACT, precision=HIGHEST, preferred_element_type=jnp.float32
     )

time: 848 us -> 857 us (1.011)
  starting transfers between devices: 0.61 us -> 10.5 us
    ppermute x0 -> x4, waiting for transfers between devices: none -> 119 us  [local(): lax.ppermute(sketch_one, 'col', [(dev, dev ^ hop) for dev in range(16)])]
    psum x1 -> x0, waiting for transfers between devices: 115 us -> none  [local(): sketch_one = lax.psum(partial_value, 'col')]
    ppermute x0 -> x4, starting transfers between devices: none -> 10.2 us  [local(): lax.ppermute(sketch_one, 'col', [(dev, dev ^ hop) for dev in range(16)])]
  transfers between devices with their start and end apart: 5 -> 8, of which waited for: 5 -> 8; matrix products, arithmetic and copies ran while one was open for 0% -> 0% of each run, Pallas kernels for 0% -> 0%
where the time goes in v2:
time: 857 us; the launch traced here: 856 us
  waiting for transfers between devices  746 us (87%)
  other arithmetic  47.9 us (6%)
  matrix products  34.7 us (4%)
  between operations  13.9 us (2%)
  starting transfers between devices  10.5 us (1%)
    psum x2, waiting for transfers between devices, sum_everywhere(): return lax.psum(gram, ('row', 'col'))  478 us
    ppermute x4, waiting for transfers between devices, local(): lax.ppermute(sketch_one, 'col', [(dev, dev ^ hop) for dev in range(16)])  119 us
    psum x1, waiting for transfers between devices, local(): pulled = lax.psum(pulled_part, 'row') / row_total  93.7 us
    reduce_scatter x1, waiting for transfers between devices, local(): lax.psum_scatter(jnp.dot(slab, pulled, precision=HIGHEST, preferred_eleme...  55.3 us
  transfers between devices with their start and end apart: 8, of which 8 were waited for; matrix products, arithmetic and copies ran while one was open for 0% of the time, Pallas kernels for 0%

profile of v2, /device:TPU:1, one launch (start us, length us, event | category | flops | bytes accessed | tf_op | source)
XLA Modules:
  0.0 856.2 jit_solution(10042275525078849779)
XLA Ops:
  7.2 1.0 copy-done
  8.2 9.9 %fusion.23 = f32[2048,128]{1,0:T(8,128)S(1)} fusion(f32[2048,1024]{1,0:T(8,128)} %param.5, f32[1024,128]{1,0:T(8,128)S(1)} %copy-done), kind=kOutput, calls=%fused_computation.34 | convolution fusion | flops 3221225472 | bytes 9961472 | tf_op jit(solution)/shard_map/dot_general | solution.py:39
  18.1 3.3 collective-permute-start
  21.5 2.3 collective-permute-done
  24.0 24.4 %collective-permute-done.1 = f32[2048,128]{1,0:T(8,128)S(1)} collective-permute-done((f32[2048,128]{1,0:T(8,128)S(1)}, f32[2048,128]{1,0:T(8,128)S(1)}, u32[]{:S(2)}, u32[]{:S(2)}) %collective-permute-start.1) | collective-permute-done | bytes 1048608 | tf_op jit(solution)/shard_map/ppermute | solution.py:44
  48.4 1.7 collective-permute-start.2
  50.1 46.5 %collective-permute-done.2 = f32[2048,128]{1,0:T(8,128)S(1)} collective-permute-done((f32[2048,128]{1,0:T(8,128)S(1)}, f32[2048,128]{1,0:T(8,128)S(1)}, u32[]{:S(2)}, u32[]{:S(2)}) %collective-permute-start.2) | collective-permute-done | bytes 1048608 | tf_op jit(solution)/shard_map/ppermute | solution.py:44
  96.8 5.1 collective-permute-start.3
  101.8 45.5 %collective-permute-done.3 = f32[2048,128]{1,0:T(8,128)S(1)} collective-permute-done((f32[2048,128]{1,0:T(8,128)S(1)}, f32[2048,128]{1,0:T(8,128)S(1)}, u32[]{:S(2)}, u32[]{:S(2)}) %collective-permute-start.3) | collective-permute-done | bytes 1048608 | tf_op jit(solution)/shard_map/ppermute | solution.py:44
  147.3 5.5 convolution_bitcast_fusion.1
  153.0 93.7 %all-reduce.4.cloned.1.call-done = f32[1024,128]{0,1:T(8,128)} async-done(((f32[1024,128]{0,1:T(8,128)}), f32[1024,128]{0,1:T(8,128)}) %all-reduce.4.cloned.1.call-update) | async-done | bytes 524304 | tf_op jit(solution)/shard_map/psum | solution.py:50
  246.7 13.0 %convolution_bitcast_fusion = f32[2048,128]{0,1:T(8,128)} fusion(f32[2048,1024]{1,0:T(8,128)} %param.5, f32[1024,128]{0,1:T(8,128)} %all-reduce.4.cloned.1.call-done), kind=kOutput, calls=%fused_computation | convolution fusion | flops 3221356544 | bytes 9961472 | tf_op jit(solution)/shard_map/dot_general | solution.py:52
  259.7 55.3 %reduce-scatter.2.cloned.1.call-done = f32[128,128]{0,1:T(8,128)} async-done(((f32[2048,128]{0,1:T(8,128)}), f32[128,128]{0,1:T(8,128)}) %reduce-scatter.2.cloned.1.call-update) | async-done | bytes 65552 | tf_op jit(solution)/shard_map/reduce_scatter | solution.py:51
  315.1 1.8 fusion.24
  316.9 243.7 %all-reduce.6.cloned.1.call-done = f32[128,128]{0,1:T(8,128)} async-done(((f32[128,128]{0,1:T(8,128)}), f32[128,128]{0,1:T(8,128)}) %all-reduce.6.cloned.1.call-update) | async-done | bytes 65552 | tf_op jit(solution)/shard_map/psum | solution.py:33
  560.6 0.9 copy.5
  562.4 11.7 %cholesky.44 = f32[128,128]{1,0:T(8,128)S(1)} custom-call(f32[128,128]{1,0:T(8,128)S(1)} %fusion.7), custom_call_target="Cholesky" | custom-call | tf_op jit(solution)/shard_map/jit(cholesky)/cholesky | solution.py:18
  575.5 9.8 %custom-call.6 = f32[1,128,128]{1,2,0:T(8,128)S(1)} custom-call(f32[1,128,128]{2,1,0:T(8,128)S(1)} %fusion.11), custom_call_target="InvertDiagBlocksLowerTriangular" | custom-call | tf_op jit(solution)/shard_map/triangular_solve/custom-call.0 | solution.py:19
  585.3 1.1 convolution_bitcast_fusion.3
  587.3 234.2 %all-reduce.8.cloned.1.call-done = f32[128,128]{0,1:T(8,128)} async-done(((f32[128,128]{0,1:T(8,128)}), f32[128,128]{0,1:T(8,128)}) %all-reduce.8.cloned.1.call-update) | async-done | bytes 65552 | tf_op jit(solution)/shard_map/psum | solution.py:33
  821.6 0.9 copy.7
  823.4 11.7 %cholesky.55 = f32[128,128]{1,0:T(8,128)S(1)} custom-call(f32[128,128]{1,0:T(8,128)S(1)} %fusion.5), custom_call_target="Cholesky" | custom-call | tf_op jit(solution)/shard_map/jit(cholesky)/cholesky | solution.py:22
  835.9 2.3 convolution_multiply_fusion
  838.8 9.8 %custom-call.7 = f32[1,128,128]{1,2,0:T(8,128)S(1)} custom-call(f32[1,128,128]{2,1,0:T(8,128)S(1)} %select_bitcast_fusion), custom_call_target="InvertDiagBlocksLowerTriangular" | custom-call | tf_op jit(solution)/shard_map/triangular_solve/custom-call.0 | solution.py:23
  (26 shorter events, 7.3 us)
Async XLA Ops:
  7.2 1.0 copy-start
  7.2 239.5 %all-reduce.4.cloned.1.call-start = ((), (), s32[]{:S(2)}) async-start(), calls=%async_computation.1 | async-start | bytes 1048576 | tf_op jit(solution)/shard_map/psum | solution.py:50
  8.2 139.1 %copy-start.1 = (f32[2048,1024]{1,0:T(8,128)S(1)}, f32[2048,1024]{1,0:T(8,128)}, u32[]{:S(2)}) copy-start(f32[2048,1024]{1,0:T(8,128)} %param.5) | copy-start | bytes 25165828
  18.1 5.6 collective-permute-start
  23.9 24.5 %collective-permute-start.1 = (f32[2048,128]{1,0:T(8,128)S(1)}, f32[2048,128]{1,0:T(8,128)S(1)}, u32[]{:S(2)}, u32[]{:S(2)}) collective-permute-start(f32[2048,128]{1,0:T(8,128)S(1)} %add.28), channel_id=1, source_target_pairs={{0,2},{1,3},{2,0},{3,1},{4,6},{5,7},{6,4},{7,5},{8,10},{9,11},{10,... | collective-permute-start | bytes 3145736 | tf_op jit(solution)/shard_map/ppermute | solution.py:44
  48.4 48.2 %collective-permute-start.2 = (f32[2048,128]{1,0:T(8,128)S(1)}, f32[2048,128]{1,0:T(8,128)S(1)}, u32[]{:S(2)}, u32[]{:S(2)}) collective-permute-start(f32[2048,128]{1,0:T(8,128)S(1)} %add.29), channel_id=1, source_target_pairs={{0,4},{1,5},{2,6},{3,7},{4,0},{5,1},{6,2},{7,3},{8,12},{9,13},{10,... | collective-permute-start | bytes 3145736 | tf_op jit(solution)/shard_map/ppermute | solution.py:44
  96.8 50.5 %collective-permute-start.3 = (f32[2048,128]{1,0:T(8,128)S(1)}, f32[2048,128]{1,0:T(8,128)S(1)}, u32[]{:S(2)}, u32[]{:S(2)}) collective-permute-start(f32[2048,128]{1,0:T(8,128)S(1)} %add.30), channel_id=1, source_target_pairs={{0,8},{1,9},{2,10},{3,11},{4,12},{5,13},{6,14},{7,15},{8,0},{9,1},... | collective-permute-start | bytes 3145736 | tf_op jit(solution)/shard_map/ppermute | solution.py:44
  152.8 162.3 %reduce-scatter.2.cloned.1.call-start = ((), (), s32[]{:S(2)}) async-start(), calls=%async_computation.2 | async-start | bytes 1114112 | tf_op jit(solution)/shard_map/reduce_scatter | solution.py:51
  259.7 301.0 %all-reduce.6.cloned.1.call-start = ((), (), s32[]{:S(2)}) async-start(), calls=%async_computation.3 | async-start | bytes 131072 | tf_op jit(solution)/shard_map/psum | solution.py:33
  316.9 504.7 %all-reduce.8.cloned.1.call-start = ((), (), s32[]{:S(2)}) async-start(), calls=%async_computation.4 | async-start | bytes 131072 | tf_op jit(solution)/shard_map/psum | solution.py:33
Sparse Core Ops, SparseCore 0:
  152.9 93.7 all-reduce.3
  259.8 55.2 reduce-scatter.1
  321.1 239.4 all-reduce.5
  587.5 234.0 all-reduce.7
